TPU v7x, 512 devices: a whole 4x8x8 slice. The times are simulated.
512 devices in a mesh: rows: 32 (over x, y), depth: 16 (over z, core).
Axes of the slice: x: 4, y: 8, z: 8, core: 2. Of those that a mesh axis runs over, the one named last changes fastest.
Arguments:
- left_factors: bfloat16 [32, 32, 2048, 128], P('rows', 'depth'), may hold values from -0.125 to 0.125
- right_factors: bfloat16 [32, 32, 2048, 128], P('rows', 'depth'), may hold values from -0.125 to 0.125
- probe_matrix: bfloat16 [2048, 128], replicated, may hold values from -6 to 6
- tile_list: int32 [32, 4], replicated, may hold values from 0 to 31, all different within a row
Outputs:
- basis: float32 [32, 4, 2048, 128], P('rows', None, 'depth')
- chol_factor: float32 [32, 4, 128, 128], P('rows')
Inputs may be any that keep to these rules, and one draw needn't show every extreme that they name: `tile_list`: each row holds 4 different tile rows, and every tile row is named by some row.
All inputs are finite; a program needn't handle non-finite values.
Results may differ from a plain program's by a relative error of at most 0.0058.
Values may be sent and summed in bfloat16 or wider, within the bound.
A program may use at most 64 MiB of HBM per device.

v0:
```python
import math
import jax
import jax.numpy as jnp
from jax import lax
from jax.sharding import PartitionSpec as P


def on_device(left_factors, right_factors, probe_matrix, tile_list):
    left_own = left_factors[0]
    right_own = right_factors[0]
    panels, tile_size, rank_size = left_own.shape
    scale = math.sqrt(float(tile_size))
    image = jnp.einsum(
        "pbk,bl->pkl", left_own, probe_matrix, preferred_element_type=jnp.float32
    ).astype(jnp.bfloat16)
    sketch_rows = jnp.einsum(
        "pbk,pkl->pbl", right_own, image, preferred_element_type=jnp.float32
    ).astype(jnp.bfloat16)
    sliced = lax.all_to_all(sketch_rows[:, None], "rows", split_axis=2, concat_axis=1, tiled=True)
    readers_order = jnp.transpose(tile_list)
    outgoing = jnp.take(sliced, readers_order, axis=1)
    arrived = lax.all_to_all(outgoing, "rows", split_axis=2, concat_axis=2, tiled=True)
    listed = arrived.shape[1]
    arrived = arrived.reshape(panels, listed, tile_size, rank_size)
    coupling = jnp.einsum(
        "pbk,ptbl->tpkl", right_own, arrived, preferred_element_type=jnp.float32
    ).astype(jnp.bfloat16)
    partial_sketch = jnp.einsum(
        "pbk,tpkl->tbl", left_own, coupling, preferred_element_type=jnp.float32
    )
    block_rows = tile_size // lax.axis_size("depth")
    total = lax.psum(partial_sketch, "depth")
    gram = jnp.einsum("tbk,tbl->tkl", total, total, precision=lax.Precision.HIGHEST)
    start = lax.axis_index("depth") * block_rows
    own_rows = lax.dynamic_slice_in_dim(total, start, block_rows, 1)
    lower = jnp.linalg.cholesky(gram)
    solved = jax.scipy.linalg.solve_triangular(
        lower, jnp.transpose(own_rows, (0, 2, 1)), lower=True
    )
    basis = jnp.transpose(solved, (0, 2, 1)) * scale
    return (basis[None], (lower / scale)[None])


def solution(mesh):
    in_specs = (P("rows", "depth", None, None), P("rows", "depth", None, None), P(), P())
    out_specs = (P("rows", None, "depth", None), P("rows", None, None, None))
    return jax.shard_map(
        on_device, mesh=mesh, in_specs=in_specs, out_specs=out_specs, check_vma=False
    )
```

profile of v0, /device:TPU:1, one launch (start us, length us, event | category | flops | bytes accessed | tf_op | source)
XLA Modules:
  0.0 398.3 jit_solution(8953928017421091047)
XLA Ops:
  7.2 0.0 copy-start
  7.2 1.2 copy-done
  8.4 2.3 fusion.3
  10.7 2.0 copy.31
  12.7 10.5 %all-to-all-start = ((bf16[2,1,2048,128]{3,0,1,2:T(2,128)(2,1)}), bf16[2,1,2048,128]{3,0,1,2:T(2,128)(2,1)S(1)}, u32[]{:S(2)}, u32[]{:S(2)}) async-start(bf16[2,1,2048,128]{3,0,1,2:T(2,128)(2,1)} %copy.31), calls=%async_computation | async-start | bytes 2097152 | tf_op jit(solution)/shard_map/all_to_all | solution.py:19
  23.2 0.0 all-reduce.2.cloned.1.call-start
  23.3 0.1 reshape.29
  23.4 0.1 copy.28
  23.5 24.3 %all-to-all-done = bf16[2,1,2048,128]{3,0,1,2:T(2,128)(2,1)S(1)} async-done(((bf16[2,1,2048,128]{3,0,1,2:T(2,128)(2,1)}), bf16[2,1,2048,128]{3,0,1,2:T(2,128)(2,1)S(1)}, u32[]{:S(2)}, u32[]{:S(2)}) %all-to-all-start) | async-done | bytes 1048608 | tf_op jit(solution)/shard_map/all_to_all | solution.py:19
  47.8 0.1 copy.32
  48.0 3.0 gather_fusion
  51.0 2.5 fusion.2
  53.5 100.6 %all_to_all.17 = bf16[2,4,32,64,128]{4,3,1,0,2:T(8,128)(2,1)S(1)} all-to-all(bf16[2,4,32,64,128]{4,3,1,0,2:T(8,128)(2,1)S(1)} %fusion.2), channel_id=1, replica_groups=mesh['rows'=32,'depth'=16] {'rows'}, dimensions={2} | all-to-all | bytes 8388608 | tf_op jit(solution)/shard_map/all_to_all | solution.py:22
  154.1 2.9 copy.34
  157.0 6.1 %convolution_bitcast_fusion = f32[4,2048,128]{1,2,0:T(8,128)} fusion(bf16[1,2,2048,128]{3,2,1,0:T(8,128)(2,1)S(1)} %copy-done, bf16[2,4,2048,128]{3,2,1,0:T(8,128)(2,1)} %bitcast.58, bf16[1,2,2048,128]{3,2,1,0:T(8,128)(2,1)S(1)} %copy-done.1), kind=kOutput, calls=%fused_computation.5 | convolution fusion | flops 1073872896 | bytes 10485760 | tf_op jit(solution)/shard_map/pbk,tpkl->tbl/dot_general | solution.py:28
  163.2 0.0 all-reduce.2.cloned.1.call-update
  163.2 131.2 %all-reduce.2.cloned.1.call-done = f32[4,2048,128]{1,2,0:T(8,128)} async-done(((f32[4,2048,128]{1,2,0:T(8,128)}), f32[4,2048,128]{1,2,0:T(8,128)}) %all-reduce.2.cloned.1.call-update) | async-done | bytes 4194320 | tf_op jit(solution)/shard_map/psum | solution.py:32
  294.5 7.4 %fusion.26 = f32[4,128,128]{2,1,0:T(8,128)S(1)} fusion(f32[4,2048,128]{1,2,0:T(8,128)} %all-reduce.2.cloned.1.call-done), kind=kOutput, calls=%fused_computation.33 | convolution fusion | flops 1610612736 | bytes 4456448 | tf_op jit(solution)/shard_map/tbk,tbl->tkl/dot_general | solution.py:33
  301.9 0.1 copy.37
  302.0 46.9 %custom-call.8 = f32[4,128,128]{2,1,0:T(8,128)S(1)} custom-call(f32[4,128,128]{2,1,0:T(8,128)S(1)} %fusion.23), custom_call_target="Cholesky" | custom-call | tf_op jit(solution)/shard_map/jit(cholesky)/cholesky | solution.py:36
  349.0 0.1 compare_reduce_fusion
  349.1 0.8 multiply_bitcast_fusion
  349.9 39.3 %custom-call.9 = f32[4,1,128,128]{2,3,1,0:T(8,128)S(1)} custom-call(f32[4,1,128,128]{3,2,1,0:T(8,128)S(1)} %get-tuple-element.3), custom_call_target="InvertDiagBlocksLowerTriangular" | custom-call | tf_op jit(solution)/shard_map/jit(_solve_triangular)/vmap()/triangular_solve | solution.py:37
  389.2 2.3 fusion.10
  (11 shorter events, 0.1 us)
Async XLA Ops:
  7.2 1.2 copy-start
  8.4 14.8 %copy-start.2 = (s32[32,4]{0,1:T(4,128)S(1)}, s32[32,4]{0,1:T(4,128)}, u32[]{:S(2)}) copy-start(s32[32,4]{0,1:T(4,128)} %param.7) | copy-start | bytes 1540
  12.7 35.1 %all-to-all-start = ((bf16[2,1,2048,128]{3,0,1,2:T(2,128)(2,1)}), bf16[2,1,2048,128]{3,0,1,2:T(2,128)(2,1)S(1)}, u32[]{:S(2)}, u32[]{:S(2)}) async-start(bf16[2,1,2048,128]{3,0,1,2:T(2,128)(2,1)} %copy.31), calls=%async_computation | async-start | bytes 2097152 | tf_op jit(solution)/shard_map/all_to_all | solution.py:19
  23.2 271.3 %all-reduce.2.cloned.1.call-start = ((), (), s32[]{:S(2)}) async-start(), calls=%async_computation.2 | async-start | bytes 8388608 | tf_op jit(solution)/shard_map/psum | solution.py:32
  154.1 3.0 copy-start.1
Sparse Core Ops, SparseCore 0:
  163.3 131.1 all-reduce.1
where the time goes:
time: 399 us; the launch traced here: 398 us
  waiting for transfers between devices  156 us (39%)
  blocking collectives  101 us (25%)
  other arithmetic  89.8 us (23%)
  matrix products  18.1 us (5%)
  between operations  14.1 us (4%)
  starting transfers between devices  10.5 us (3%)
  local copies, waits for them, and re-layouts  9.65 us (2%)
    psum x1, waiting for transfers between devices, on_device(): total = lax.psum(partial_sketch, 'depth')  131 us
    all_to_all x1, blocking collectives, on_device(): lax.all_to_all(outgoing, 'rows', split_axis=2, concat_axis=2, tiled=True)  101 us
    another operation x4, other arithmetic, on_device(): lower = jnp.linalg.cholesky(gram)  47.1 us
    another operation x2, other arithmetic, on_device(): jax.scipy.linalg.solve_triangular(lower, jnp.transpose(own_rows, (0, 2, 1...  39.3 us
    all_to_all x1, waiting for transfers between devices, on_device(): lax.all_to_all(sketch_rows[:, None], 'rows', split_axis=2, concat_axis=1,...  24.3 us
    all_to_all x1, starting transfers between devices, on_device(): lax.all_to_all(sketch_rows[:, None], 'rows', split_axis=2, concat_axis=1,...  10.5 us
  transfers between devices with their start and end apart: 2, of which 2 were waited for; matrix products, arithmetic and copies ran while one was open for 0% of the time, Pallas kernels for 0%

commit v1 on v0

--- a/solution.py
+++ b/solution.py
@@ -3,6 +3,14 @@
 import jax.numpy as jnp
 from jax import lax
 from jax.sharding import PartitionSpec as P
+
+
+def added_up(x, axis):
+    size, total = (lax.axis_size(axis), x)
+    for far in [1 << k for k in range(size.bit_length() - 1)]:
+        route = [(i, i ^ far) for i in range(size)]
+        total = total + lax.ppermute(total, axis, route)
+    return total
 
 
 def on_device(left_factors, right_factors, probe_matrix, tile_list):
@@ -29,7 +37,7 @@
         "pbk,tpkl->tbl", left_own, coupling, preferred_element_type=jnp.float32
     )
     block_rows = tile_size // lax.axis_size("depth")
-    total = lax.psum(partial_sketch, "depth")
+    total = added_up(partial_sketch, "depth")
     gram = jnp.einsum("tbk,tbl->tkl", total, total, precision=lax.Precision.HIGHEST)
     start = lax.axis_index("depth") * block_rows
     own_rows = lax.dynamic_slice_in_dim(total, start, block_rows, 1)

time: 399 us -> 747 us (1.87)
  waiting for transfers between devices: 156 us -> 482 us
  starting transfers between devices: 10.5 us -> 35.4 us
  between operations: 14.1 us -> 0.79 us
  other arithmetic: 89.8 us -> 101 us
    ppermute x0 -> x4, waiting for transfers between devices: none -> 458 us  [added_up(): total = total + lax.ppermute(total, axis, route)]
    psum x1 -> x0, waiting for transfers between devices: 131 us -> none  [on_device(): total = lax.psum(partial_sketch, 'depth')]
    ppermute x0 -> x4, starting transfers between devices: none -> 24.9 us  [added_up(): total = total + lax.ppermute(total, axis, route)]
    add x0 -> x4, other arithmetic: none -> 10.9 us  [added_up(): total = total + lax.ppermute(total, axis, route)]
  transfers between devices with their start and end apart: 2 -> 5, of which waited for: 2 -> 5; matrix products, arithmetic and copies ran while one was open for 0% -> 0% of each run, Pallas kernels for 0% -> 0%
where the time goes in v1:
time: 747 us; the launch traced here: 746 us
  waiting for transfers between devices  482 us (65%)
  other arithmetic  101 us (14%)
  blocking collectives  101 us (14%)
  starting transfers between devices  35.4 us (5%)
  matrix products  14.7 us (2%)
  local copies, waits for them, and re-layouts  11.5 us (2%)
    ppermute x4, waiting for transfers between devices, added_up(): total = total + lax.ppermute(total, axis, route)  458 us
    all_to_all x1, blocking collectives, on_device(): lax.all_to_all(outgoing, 'rows', split_axis=2, concat_axis=2, tiled=True)  101 us
    another operation x4, other arithmetic, on_device(): lower = jnp.linalg.cholesky(gram)  47.1 us
    another operation x2, other arithmetic, on_device(): jax.scipy.linalg.solve_triangular(lower, jnp.transpose(own_rows, (0, 2, 1...  39.3 us
    ppermute x4, starting transfers between devices, added_up(): total = total + lax.ppermute(total, axis, route)  24.9 us
    all_to_all x1, waiting for transfers between devices, on_device(): lax.all_to_all(sketch_rows[:, None], 'rows', split_axis=2, concat_axis=1,...  24.4 us
  transfers between devices with their start and end apart: 5, of which 5 were waited for; matrix products, arithmetic and copies ran while one was open for 0% of the time, Pallas kernels for 0%

profile of v1, /device:TPU:1, one launch (start us, length us, event | category | flops | bytes accessed | tf_op | source)
XLA Modules:
  0.0 745.9 jit_solution(7146306681799015975)
XLA Ops:
  1.9 2.3 fusion.3
  4.2 2.0 copy.31
  6.2 10.5 %all-to-all-start = ((bf16[2,1,2048,128]{3,0,1,2:T(2,128)(2,1)}), bf16[2,1,2048,128]{3,0,1,2:T(2,128)(2,1)S(1)}, u32[]{:S(2)}, u32[]{:S(2)}) async-start(bf16[2,1,2048,128]{3,0,1,2:T(2,128)(2,1)} %copy.31), calls=%async_computation | async-start | bytes 2097152 | tf_op jit(solution)/shard_map/all_to_all | solution.py:27
  16.9 24.4 %all-to-all-done = bf16[2,1,2048,128]{3,0,1,2:T(2,128)(2,1)S(1)} async-done(((bf16[2,1,2048,128]{3,0,1,2:T(2,128)(2,1)}), bf16[2,1,2048,128]{3,0,1,2:T(2,128)(2,1)S(1)}, u32[]{:S(2)}, u32[]{:S(2)}) %all-to-all-start) | async-done | bytes 1048608 | tf_op jit(solution)/shard_map/all_to_all | solution.py:27
  41.4 3.0 gather_fusion
  44.4 2.5 fusion.2
  47.0 100.6 %all_to_all.17 = bf16[2,4,32,64,128]{4,3,1,0,2:T(8,128)(2,1)S(1)} all-to-all(bf16[2,4,32,64,128]{4,3,1,0,2:T(8,128)(2,1)S(1)} %fusion.2), channel_id=1, replica_groups=mesh['rows'=32,'depth'=16] {'rows'}, dimensions={2} | all-to-all | bytes 8388608 | tf_op jit(solution)/shard_map/all_to_all | solution.py:30
  147.5 2.9 copy.34
  150.4 6.2 convolution_bitcast_fusion
  156.6 6.9 collective-permute-start
  163.5 7.0 collective-permute-done
  170.5 2.9 add.37
  173.4 4.0 collective-permute-start.1
  177.4 90.6 %collective-permute-done.1 = f32[4,2048,128]{1,2,0:T(8,128)S(1)} collective-permute-done((f32[4,2048,128]{1,2,0:T(8,128)S(1)}, f32[4,2048,128]{1,2,0:T(8,128)S(1)}, u32[]{:S(2)}, u32[]{:S(2)}) %collective-permute-start.1) | collective-permute-done | bytes 4194336 | tf_op jit(solution)/shard_map/ppermute | solution.py:12
  269.2 5.8 collective-permute-start.2
  275.0 180.0 %collective-permute-done.2 = f32[4,2048,128]{1,2,0:T(8,128)S(1)} collective-permute-done((f32[4,2048,128]{1,2,0:T(8,128)S(1)}, f32[4,2048,128]{1,2,0:T(8,128)S(1)}, u32[]{:S(2)}, u32[]{:S(2)}) %collective-permute-start.2) | collective-permute-done | bytes 4194336 | tf_op jit(solution)/shard_map/ppermute | solution.py:12
  455.0 2.7 add.39
  457.7 8.2 %collective-permute-start.3 = (f32[4,2048,128]{1,2,0:T(8,128)}, f32[4,2048,128]{1,2,0:T(8,128)}, u32[]{:S(2)}, u32[]{:S(2)}) collective-permute-start(f32[4,2048,128]{1,2,0:T(8,128)} %add.39), channel_id=1, source_target_pairs={{0,8},{1,9},{2,10},{3,11},{4,12},{5,13},{6,14},{7,15},{8,0},{9,1},... | collective-permute-start | bytes 12582920 | tf_op jit(solution)/shard_map/ppermute | solution.py:12
  465.9 180.2 %collective-permute-done.3 = f32[4,2048,128]{1,2,0:T(8,128)} collective-permute-done((f32[4,2048,128]{1,2,0:T(8,128)}, f32[4,2048,128]{1,2,0:T(8,128)}, u32[]{:S(2)}, u32[]{:S(2)}) %collective-permute-start.3) | collective-permute-done | bytes 4194336 | tf_op jit(solution)/shard_map/ppermute | solution.py:12
  646.2 4.2 add.40
  652.3 3.9 fusion.26
  656.4 46.9 %custom-call.8 = f32[4,128,128]{2,1,0:T(8,128)S(1)} custom-call(f32[4,128,128]{2,1,0:T(8,128)S(1)} %fusion.23), custom_call_target="Cholesky" | custom-call | tf_op jit(solution)/shard_map/jit(cholesky)/cholesky | solution.py:44
  704.3 39.3 %custom-call.9 = f32[4,1,128,128]{2,3,1,0:T(8,128)S(1)} custom-call(f32[4,1,128,128]{3,2,1,0:T(8,128)S(1)} %get-tuple-element.3), custom_call_target="InvertDiagBlocksLowerTriangular" | custom-call | tf_op jit(solution)/shard_map/jit(_solve_triangular)/vmap()/triangular_solve | solution.py:45
  743.6 2.3 fusion.10
  (22 shorter events, 5.8 us)
Async XLA Ops:
  0.6 1.2 copy-start
  1.9 14.8 %copy-start.3 = (s32[32,4]{0,1:T(4,128)S(1)}, s32[32,4]{0,1:T(4,128)}, u32[]{:S(2)}) copy-start(s32[32,4]{0,1:T(4,128)} %param.7) | copy-start | bytes 1540
  6.2 35.1 %all-to-all-start = ((bf16[2,1,2048,128]{3,0,1,2:T(2,128)(2,1)}), bf16[2,1,2048,128]{3,0,1,2:T(2,128)(2,1)S(1)}, u32[]{:S(2)}, u32[]{:S(2)}) async-start(bf16[2,1,2048,128]{3,0,1,2:T(2,128)(2,1)} %copy.31), calls=%async_computation | async-start | bytes 2097152 | tf_op jit(solution)/shard_map/all_to_all | solution.py:27
  147.5 2.9 copy-start.2
  156.6 13.9 %collective-permute-start = (f32[4,2048,128]{1,2,0:T(8,128)}, f32[4,2048,128]{1,2,0:T(8,128)S(1)}, u32[]{:S(2)}, u32[]{:S(2)}) collective-permute-start(f32[4,2048,128]{1,2,0:T(8,128)} %convolution_bitcast_fusion), channel_id=1, source_target_pairs={{0,1},{1,0},{2,3},{3,2},{4,5},{5,4},{6,7},{7,6},{8,9},{9,8},{10,11... | collective-permute-start | bytes 12582920 | tf_op jit(solution)/shard_map/ppermute | solution.py:12
  173.4 94.6 %collective-permute-start.1 = (f32[4,2048,128]{1,2,0:T(8,128)S(1)}, f32[4,2048,128]{1,2,0:T(8,128)S(1)}, u32[]{:S(2)}, u32[]{:S(2)}) collective-permute-start(f32[4,2048,128]{1,2,0:T(8,128)S(1)} %add.37), channel_id=1, source_target_pairs={{0,2},{1,3},{2,0},{3,1},{4,6},{5,7},{6,4},{7,5},{8,10},{9,11},{10,... | collective-permute-start | bytes 12582920 | tf_op jit(solution)/shard_map/ppermute | solution.py:12
  269.2 185.9 %collective-permute-start.2 = (f32[4,2048,128]{1,2,0:T(8,128)S(1)}, f32[4,2048,128]{1,2,0:T(8,128)S(1)}, u32[]{:S(2)}, u32[]{:S(2)}) collective-permute-start(f32[4,2048,128]{1,2,0:T(8,128)S(1)} %add.38), channel_id=1, source_target_pairs={{0,4},{1,5},{2,6},{3,7},{4,0},{5,1},{6,2},{7,3},{8,12},{9,13},{10,... | collective-permute-start | bytes 12582920 | tf_op jit(solution)/shard_map/ppermute | solution.py:12
  457.7 188.5 %collective-permute-start.3 = (f32[4,2048,128]{1,2,0:T(8,128)}, f32[4,2048,128]{1,2,0:T(8,128)}, u32[]{:S(2)}, u32[]{:S(2)}) collective-permute-start(f32[4,2048,128]{1,2,0:T(8,128)} %add.39), channel_id=1, source_target_pairs={{0,8},{1,9},{2,10},{3,11},{4,12},{5,13},{6,14},{7,15},{8,0},{9,1},... | collective-permute-start | bytes 12582920 | tf_op jit(solution)/shard_map/ppermute | solution.py:12
  650.4 1.9 copy-start.1
